TPU v7x, 128 devices: a whole 4x4x4 slice. The times are simulated.
128 devices in a mesh: req: 16 (over x, z), tp: 8 (over y, core).
Axes of the slice: x: 4, y: 4, z: 4, core: 2. Of those that a mesh axis runs over, the one named last changes fastest.
Arguments:
- tokens: int32 [4, 384], replicated, may hold values from 0 to 32767
- finish: int32 [4, 384], replicated, may hold values from 0 to 1, as said below
- holder: int32 [4, 384], replicated, may hold values from 0 to 15, as said below
- slot_index: int32 [4, 384], replicated, may hold values from 0 to 63, as said below
- embedding: bfloat16 [32768, 8192], P('tp', 'req'), may hold values from -12 to 12, as said below
- norm_gain: float32 [8192], P('req'), may hold values from 0.5 to 1.5
- proj_inner: bfloat16 [8192, 16384], P('req', 'tp'), may hold values from -0.0625 to 0.0625
- proj_gate: bfloat16 [8192, 16384], P('req', 'tp'), may hold values from -0.0625 to 0.0625
- conv_weight: float32 [4, 16384], P(None, 'tp'), may hold values from -2.5 to 2.5
- conv_bias: float32 [16384], P('tp'), may hold values from -2.5 to 2.5
- proj_low: bfloat16 [16384, 512], P('tp'), may hold values from -0.046875 to 0.046875
- proj_select: bfloat16 [32, 16384], P(None, 'tp'), may hold values from -0.046875 to 0.046875
- proj_dt: bfloat16 [512, 16384], P(None, 'tp'), may hold values from -0.25 to 0.25
- dt_bias: float32 [16384], P('tp'), may hold values from -5 to -1.5
- decay_log: float32 [16, 16384], P(None, 'tp'), may hold values from 0 to 2.77
- skip_gain: float32 [16384], P('tp'), may hold values from 0.5 to 1.5
- proj_out: bfloat16 [16384, 8192], P('tp', 'req'), may hold values from -0.046875 to 0.046875
- state_codes: bfloat16 [384, 16, 16384], P('req', None, 'tp'), may hold values from -1 to 1
- state_scales: bfloat16 [384, 128], P('req', 'tp'), may hold values from 0.099609375 to 1
- conv_state: bfloat16 [384, 3, 16384], P('req', None, 'tp'), may hold values from -6 to 6
Outputs:
- mixed: bfloat16 [4, 384, 8192], P(None, None, 'req')
- next_codes: bfloat16 [384, 16, 16384], P('req', None, 'tp')
- next_scales: bfloat16 [384, 128], P('req', 'tp')
- next_window: bfloat16 [384, 3, 16384], P('req', None, 'tp')
- cache_codes: bfloat16 [1024, 16, 16384], P('req', None, 'tp')
- cache_scales: bfloat16 [1024, 128], P('req', 'tp')
- cache_window: bfloat16 [1024, 3, 16384], P('req', None, 'tp')
Inputs may be any that keep to these rules, and one draw needn't show every extreme that they name: `finish`: 1 where the turn ends; in every step, among the rows of one device (aligned blocks of 24 requests), at most 2 finishing requests name the same holder, and this bound is reached. Where finish is 1, the holder of the saved state. Each holder receives at most 64 saves over all steps, and some holder receives exactly 64; other holders may receive far fewer. Where finish is 0 the entry is arbitrary. Where finish is 1, each pair of holder and slot_index occurs at most once over all steps and requests; where finish is 0 the entry is arbitrary. `embedding`: token vectors.
All inputs are finite; a program needn't handle non-finite values.
Results may differ from a plain program's by a relative error of at most 0.035.
Values may be sent and summed in bfloat16 or wider, within the bound.
A program may use at most 128 MiB of HBM per device.

v0:
```python
import functools

import jax
import jax.numpy as jnp
from jax import lax
from jax.experimental import pallas as pl
from jax.experimental.pallas import tpu as pltpu
from jax.sharding import PartitionSpec as P

D = 8192
STATE = 16
PAGE = 128
STEPS = 4
CAP = 2
ROWS = 24
BLOCKS = 16
BROWS = STEPS * ROWS
SLOTS = 64
INNER = 2048
HALF = INNER // 2
FEATS = 512
WIDE = 512
RANK = 512
PAIRS = STEPS * CAP
F32 = jnp.float32
BF16 = jnp.bfloat16
MESH = pl.DeviceIdType.MESH
VMEM_LIMIT = 62 * 1024 * 1024


def rcopy(src, dst, send, recv, dev):
    return pltpu.make_async_remote_copy(
        src_ref=src, dst_ref=dst, send_sem=send, recv_sem=recv, device_id=dev, device_id_type=MESH
    )


def mod4(v):
    return lax.rem(v + 8, 4)


def dot(a, b):
    return jnp.dot(a, b, preferred_element_type=F32)


def greet(devices):
    barrier = pltpu.get_barrier_semaphore()
    for dev in devices:
        pl.semaphore_signal(barrier, inc=1, device_id=dev, device_id_type=MESH)
    pl.semaphore_wait(barrier, len(devices))


def tp_scratch(rows):
    return (
        [pltpu.VMEM((4, 2, rows, FEATS), BF16)] * 2
        + [pltpu.VMEM((4, 2, rows, FEATS), F32)]
        + [pltpu.VMEM((2, rows, FEATS), BF16)] * 6
        + [pltpu.SemaphoreType.DMA((20,)), pltpu.SemaphoreType.DMA((20,))]
    )


TP_SCRATCH = tp_scratch(BROWS)


def tp_partners():
    r, t = lax.axis_index("req"), lax.axis_index("tp")
    y, c = lax.div(t, 2), lax.rem(t, 2)
    return [(r, y * 2 + 1 - c), (r, mod4(y + 1) * 2 + c), (r, mod4(y - 1) * 2 + c)]


def tp_steps(get, total, bufs):
    half_s, half_r, part, far_s, far_r, dir_s, dir_r, com_s, com_r, ss, rs = bufs
    t = lax.axis_index("tp")
    y, c = lax.div(t, 2), lax.rem(t, 2)
    core, up, down = tp_partners()
    order = [mod4(y + 2), mod4(y + 1), mod4(y - 1), y]
    sent = []

    def send(src, dst, n, dev):
        copy = rcopy(src, dst, ss.at[n], rs.at[n], dev)
        copy.start()
        sent.append(copy)

    def arrived(ref, n):
        rcopy(ref, ref, ss.at[n], rs.at[n], core).wait_recv()

    def pair(group, yy):
        return pl.ds(2 * (group * 4 + yy), 2)

    for k in range(4):
        half_s[k] = get((1 - c) * 4 + order[k]).astype(BF16)
        send(half_s.at[k], half_r.at[k], k, core)
    for k in range(4):
        mine = get(c * 4 + order[k])
        arrived(half_r.at[k], k)
        part[k] = mine + half_r[k].astype(F32)
        if k == 0:
            far_s[...] = part[0].astype(BF16)
            send(far_s.at[0], far_r.at[0], 4, up)
            send(far_s.at[1], far_r.at[1], 5, down)
        if k == 1:
            dir_s[1] = part[1, 1].astype(BF16)
            send(dir_s.at[1], dir_r.at[1], 7, up)
        if k == 2:
            dir_s[0] = part[2, 0].astype(BF16)
            send(dir_s.at[0], dir_r.at[0], 6, down)
    yield
    arrived(far_r.at[0], 4)
    com_s[0] = (part[1, 0] + far_r[0].astype(F32)).astype(BF16)
    send(com_s.at[0], com_r.at[0], 8, up)
    arrived(far_r.at[1], 5)
    com_s[1] = (part[2, 1] + far_r[1].astype(F32)).astype(BF16)
    send(com_s.at[1], com_r.at[1], 9, down)
    own = 2 * (c * 4 + y)
    for h in range(2):
        arrived(dir_r.at[h], 6 + h)
        arrived(com_r.at[h], 8 + h)
        total[own + h] = (part[3, h] + dir_r[h].astype(F32) + com_r[h].astype(F32)).astype(BF16)
    mine = total.at[pair(c, y)]
    send(mine, mine, 10, up)
    send(mine, mine, 11, down)
    send(mine, mine, 12, core)
    below = total.at[pair(c, mod4(y - 1))]
    above = total.at[pair(c, mod4(y + 1))]
    arrived(below, 10)
    first = total.at[2 * (c * 4 + mod4(y - 1))]
    send(first, first, 13, up)
    send(below, below, 15, core)
    arrived(above, 11)
    second = total.at[2 * (c * 4 + mod4(y + 1)) + 1]
    send(second, second, 14, down)
    send(above, above, 16, core)
    far = 2 * (c * 4 + mod4(y + 2))
    arrived(total.at[far], 13)
    send(total.at[far], total.at[far], 17, core)
    arrived(total.at[far + 1], 14)
    send(total.at[far + 1], total.at[far + 1], 18, core)
    arrived(total.at[pair(1 - c, y)], 12)
    arrived(total.at[pair(1 - c, mod4(y - 1))], 15)
    arrived(total.at[pair(1 - c, mod4(y + 1))], 16)
    other = 2 * ((1 - c) * 4 + mod4(y + 2))
    arrived(total.at[other], 17)
    arrived(total.at[other + 1], 18)
    for copy in sent:
        copy.wait_send()
    yield


def tp_sum(get, total, bufs):
    for _ in tp_steps(get, total, bufs):
        pass


def shift_req(axis, d):
    r, t = lax.axis_index("req"), lax.axis_index("tp")
    x, z = lax.div(r, 4), lax.rem(r, 4)
    if axis == 0:
        return (mod4(x + d) * 4 + z, t)
    return (x * 4 + mod4(z + d), t)


def req_place(axis):
    r = lax.axis_index("req")
    return lax.div(r, 4) if axis == 0 else lax.rem(r, 4)


def req_partners():
    return [shift_req(axis, d) for axis in (0, 1) for d in (1, -1)]


PROWS = BROWS // 2
FRONT_SCRATCH = (
    [
        pltpu.VMEM((2, BLOCKS, PROWS, FEATS), BF16),
        pltpu.VMEM((2, 4, 4 * PROWS, FEATS), BF16),
        pltpu.VMEM((2, 4, 4 * PROWS, FEATS), BF16),
        pltpu.VMEM((2, 4, 4 * PROWS, PAGE), F32),
    ]
    + [pltpu.VMEM((2, 2, 4, 4 * PROWS, WIDE), BF16)] * 6
    + [pltpu.VMEM((2, 2, 4, PROWS, WIDE), BF16)] * 6
    + [pltpu.VMEM((2, 2, 4, 4, PROWS, WIDE), F32)]
    + [pltpu.SemaphoreType.DMA((2, 6, 2, 4)), pltpu.SemaphoreType.DMA((2, 6, 2, 4))]
    + [pltpu.VMEM((2, 4 * PROWS, PAGE), BF16)] * 6
    + [pltpu.VMEM((2, PROWS, PAGE), BF16)] * 6
    + [pltpu.VMEM((2, 4, PROWS, PAGE), F32)]
    + [pltpu.SemaphoreType.DMA((2, 6)), pltpu.SemaphoreType.DMA((2, 6))]
)


class ScatterSum:
    def __init__(self, axis, d, partial, bufs, total, ss, rs):
        self.axes = (axis, 1 - axis)
        self.d = d
        self.partial = partial
        self.far_s, self.far_r, self.dir_s, self.dir_r, self.com_s, self.com_r = bufs[:6]
        self.far2_s, self.far2_r, self.dir2_s, self.dir2_r, self.com2_s, self.com2_r = bufs[6:]
        self.total = total
        self.ss, self.rs = ss, rs

    def copy(self, n):
        src = (self.far_s, self.dir_s, self.com_s, self.far2_s, self.dir2_s, self.com2_s)[n]
        dst = (self.far_r, self.dir_r, self.com_r, self.far2_r, self.dir2_r, self.com2_r)[n]
        d = -self.d if n % 3 == 1 else self.d
        return rcopy(src, dst, self.ss(n), self.rs(n), shift_req(self.axes[n // 3], d))

    def far(self):
        p = req_place(self.axes[0])
        self.far_s[...] = self.partial(mod4(p + 2)).astype(BF16)
        self.copy(0).start()

    def direct(self):
        p = req_place(self.axes[0])
        self.dir_s[...] = self.partial(mod4(p - self.d)).astype(BF16)
        self.copy(1).start()

    def combined(self):
        p = req_place(self.axes[0])
        mine = self.partial(mod4(p + self.d))
        self.copy(0).wait_recv()
        self.com_s[...] = (mine + self.far_r[...].astype(F32)).astype(BF16)
        self.copy(2).start()

    def own(self):
        p, q = req_place(self.axes[0]), req_place(self.axes[1])
        mine = self.partial(p)
        self.copy(1).wait_recv()
        self.copy(2).wait_recv()
        mine = mine + self.dir_r[...].astype(F32) + self.com_r[...].astype(F32)
        self.total[...] = mine.reshape(4, PROWS, mine.shape[1])
        self.far2_s[...] = self.total[mod4(q + 2)].astype(BF16)
        self.copy(3).start()
        self.dir2_s[...] = self.total[mod4(q - self.d)].astype(BF16)
        self.copy(4).start()

    def combined2(self):
        q = req_place(self.axes[1])
        self.copy(3).wait_recv()
        self.com2_s[...] = (self.total[mod4(q + self.d)] + self.far2_r[...].astype(F32)).astype(
            BF16
        )
        self.copy(5).start()

    def result(self):
        q = req_place(self.axes[1])
        self.copy(4).wait_recv()
        self.copy(5).wait_recv()
        return self.total[q] + self.dir2_r[...].astype(F32) + self.com2_r[...].astype(F32)

    def drain(self):
        for n in range(6):
            self.copy(n).wait_send()


class Front:
    def __init__(self, g, refs, out, tp_bufs, rest):
        self.g, self.out, self.tp_bufs = g, out, tp_bufs
        self.ids, self.emb, self.gain, self.w_inner, self.w_gate = refs
        self.embedded, self.lhs_x, self.lhs_z, self.squares = (ref.at[g] for ref in rest[:4])
        self.big = [ref.at[g] for ref in rest[4:17]]
        self.big_ss, self.big_rs = rest[17:19]
        small = [ref.at[g] for ref in rest[19:32]]
        small_ss, small_rs = rest[32:34]
        self.norm = ScatterSum(
            0, 1, lambda chunk: self.squares[chunk], small[:12], small[12],
            lambda n: small_ss.at[g, n], lambda n: small_rs.at[g, n],
        )

    def looked(self, ch):
        emb = self.emb
        want = self.ids[self.g, pl.ds(2 * ch, 2)].reshape(2 * PROWS, 1)
        span = 1024
        acc = jnp.zeros((2 * PROWS, FEATS), F32)
        for k in range(emb.shape[0] // span):
            lane = lax.broadcasted_iota(jnp.int32, (2 * PROWS, span), 1) + k * span
            hot = jnp.where(lane == want, 1.0, 0.0).astype(BF16)
            acc = acc + dot(hot, emb[k * span : (k + 1) * span, :])
        return acc.reshape(2, PROWS, FEATS)

    def lookup(self):
        return tp_steps(self.looked, self.embedded, self.tp_bufs)

    def spread(self):
        def body(b, carry):
            x, z = lax.div(b, 4), lax.rem(b, 4)
            rows = self.embedded[b].astype(F32)
            scaled = (rows * self.gain[...]).astype(BF16)
            along_z = pl.ds(pl.multiple_of(z * PROWS, PROWS), PROWS)
            along_x = pl.ds(pl.multiple_of(x * PROWS, PROWS), PROWS)
            self.lhs_x[x, along_z, :] = scaled
            self.lhs_z[z, along_x, :] = scaled
            self.squares[x, along_z, :] = jnp.broadcast_to(
                jnp.sum(rows * rows, axis=1, keepdims=True), (PROWS, PAGE)
            )
            return carry

        lax.fori_loop(0, BLOCKS, body, 0)

    def unit(self, ab, u):
        lhs, weight = ((self.lhs_x, self.w_inner), (self.lhs_z, self.w_gate))[ab]
        g = self.g

        def partial(chunk):
            cols = pl.ds(pl.multiple_of(u * WIDE, WIDE), WIDE)
            return dot(lhs[chunk], weight[:, cols])

        views = [ref.at[ab, u] for ref in self.big[:12]]
        return ScatterSum(
            ab, 1 - 2 * lax.rem(u, 2), partial, views, self.big[12].at[ab, u],
            lambda n: self.big_ss.at[g, n, ab, u], lambda n: self.big_rs.at[g, n, ab, u],
        )

    def each(self, step):
        step(self.norm)

        def body(u, carry):
            for ab in range(2):
                step(self.unit(ab, u))
            return carry

        lax.fori_loop(0, 4, body, 0)

    def finish(self):
        inv_rms = lax.rsqrt(self.norm.result()[:, :1] / D + 1e-05)

        def body(u, carry):
            for ab in range(2):
                cols = pl.ds(pl.multiple_of((ab * 4 + u) * WIDE, WIDE), WIDE)
                rows = slice(self.g * PROWS, (self.g + 1) * PROWS)
                self.out[rows, cols] = self.unit(ab, u).result() * inv_rms
            return carry

        lax.fori_loop(0, 4, body, 0)


PLAN, FIRST, SECOND, LAST, SIDE1, SIDE2, WHICH = 24, 0, 4, 8, 9, 13, 17
GROUP = 4 * BROWS
MOST = 32


def make_plan(events, plan):
    r = lax.axis_index("req")
    shape = (GROUP, 128)
    lane = lax.broadcasted_iota(jnp.int32, shape, 1)
    number = lax.broadcasted_iota(jnp.int32, shape, 0)
    kind, quarter = lax.rem(lane, 4), lax.div(lane, 4)
    block = lax.div(number, BROWS)
    row = lax.broadcasted_iota(jnp.int32, (GROUP, GROUP), 0)
    col = lax.broadcasted_iota(jnp.int32, (GROUP, GROUP), 1)
    earlier = col < row
    near = earlier & (lax.div(col, BROWS) == lax.div(row, BROWS))
    earlier = jnp.where(earlier, 1.0, 0.0).astype(BF16)
    near = jnp.where(near, 1.0, 0.0).astype(BF16)

    def ahead(which, mask):
        return dot(which, jnp.where(mask, 1.0, 0.0).astype(BF16)).astype(jnp.int32)

    def parts(packed):
        packed = jnp.broadcast_to(packed, shape)
        owner = jnp.bitwise_and(jnp.right_shift(packed, 6), 15)
        return packed >= 4096, owner, jnp.bitwise_and(packed, 63)

    def fold(mask, value):
        return jnp.sum(jnp.where(mask, value + 1, 0), axis=0, keepdims=True) - 1

    plan[...] = jnp.zeros_like(plan)
    need1 = jnp.zeros((1, 128), jnp.int32)
    need2 = jnp.zeros((1, 128), jnp.int32)
    for h in range(2):
        p_me, q_me = req_place(h), req_place(1 - h)
        done, owner, _ = parts(events[h, q_me])
        p_of = lax.div(owner, 4) if h == 0 else lax.rem(owner, 4)
        q_of = lax.rem(owner, 4) if h == 0 else lax.div(owner, 4)
        mask1 = done & (p_of == lane)
        rank1 = ahead(near, mask1)
        mask2 = done & (p_of == p_me) & (q_of == lane)
        rank2 = ahead(earlier, mask2)
        here = jnp.sum(jnp.where(lane == p_me, rank1, 0), axis=1, keepdims=True)
        at = block * MOST + here
        mine = block == p_me
        event = number - p_me * BROWS
        base = PLAN * h
        for d in range(4):
            rank = jnp.broadcast_to(rank1[:, d : d + 1], shape)
            mask = mine & done & (p_of == d)
            plan[base + FIRST + d : base + FIRST + d + 1, :] = fold(mask & (rank == lane), event)
            plan[base + SIDE1 + d : base + SIDE1 + d + 1, :] = fold(
                mask & (rank == quarter), kind * BROWS + event
            )
            rank = jnp.broadcast_to(rank2[:, d : d + 1], shape)
            mask = done & (p_of == p_me) & (q_of == d)
            plan[base + SECOND + d : base + SECOND + d + 1, :] = fold(mask & (rank == lane), at)
            plan[base + SIDE2 + d : base + SIDE2 + d + 1, :] = fold(
                mask & (rank == quarter), at * 4 + kind
            )
        found = jnp.zeros((1, 128), jnp.int32)
        for q in range(4):
            done, owner, slot = parts(events[h, q])
            mask = done & (owner == r)
            value = q * MOST + ahead(earlier, mask)
            found = found + fold(mask & (slot == lane), value) + 1
            p_of = lax.div(owner, 4) if h == 0 else lax.rem(owner, 4)
            leaving = jnp.where(done & (p_of == lane), 1, 0).reshape(4, BROWS, 128)
            for n in range(4):
                need1 = jnp.maximum(need1, jnp.sum(leaving[n], axis=0, keepdims=True))
            staying = jnp.where(done & (owner == lane), 1, 0)
            need2 = jnp.maximum(need2, jnp.sum(staying, axis=0, keepdims=True))
        plan[base + LAST : base + LAST + 1, :] = found - 1
    need1 = jnp.max(need1, axis=1, keepdims=True)
    need2 = jnp.max(need2, axis=1, keepdims=True)
    which = jnp.full((1, 1), len(SAVE_COUNTS) - 1, jnp.int32)
    for n in range(len(SAVE_COUNTS) - 2, -1, -1):
        few, many = SAVE_COUNTS[n]
        which = jnp.where((need1 <= few) & (need2 <= many), n, which)
    plan[WHICH : WHICH + 1, :] = jnp.broadcast_to(which, (1, 128))


TP_PAIR = tp_scratch(PROWS)


def front_kernel(ids, emb, gain, w_inner, w_gate, events, out, plan, *scratch):
    cut = len(TP_PAIR)
    refs = (ids, emb, gain, w_inner, w_gate)
    one, two = (
        Front(g, refs, out, scratch[g * cut : (g + 1) * cut], scratch[2 * cut :]) for g in range(2)
    )
    greet(tp_partners() + req_partners())
    for _ in one.lookup():
        pass
    one.spread()
    one.each(lambda s: s.far())
    one.each(lambda s: s.direct())
    lookup = two.lookup()
    next(lookup)
    one.each(lambda s: s.combined())
    next(lookup)
    two.spread()
    two.each(lambda s: s.far())
    one.each(lambda s: s.own())
    two.each(lambda s: s.direct())
    one.each(lambda s: s.combined2())
    make_plan(events, plan)
    two.each(lambda s: s.combined())
    one.finish()
    two.each(lambda s: s.own())
    two.each(lambda s: s.combined2())
    two.finish()
    one.each(lambda s: s.drain())
    two.each(lambda s: s.drain())


def vmem_call(kernel, out_shape, n_in, scratch, **params):
    spec = pl.BlockSpec(memory_space=pltpu.VMEM)
    return pl.pallas_call(
        kernel,
        out_shape=out_shape,
        in_specs=[spec] * n_in,
        out_specs=jax.tree.map(lambda _: spec, out_shape),
        scratch_shapes=scratch,
        compiler_params=pltpu.CompilerParams(vmem_limit_bytes=VMEM_LIMIT, **params),
    )


def silu(v):
    return v / (1.0 + jnp.exp(-v))


RCOLS = RANK + 128


def rank_kernel(
    sums, conv, taps, bias, w_low, w_select, w_dt, dt_bias, step, activ, select,
    pair_s, pair_r, quad_s, quad_r, full, ss, rs,
):
    r, t = lax.axis_index("req"), lax.axis_index("tp")
    y, c = lax.div(t, 2), lax.rem(t, 2)
    core = (r, y * 2 + 1 - c)
    others = [(r, mod4(y + d) * 2 + c) for d in (1, 2, 3)]
    greet([core] + others)
    for n in range(STEPS):
        total = bias[...] + jnp.zeros((ROWS, INNER), F32)
        for k in range(4):
            at = n + k
            if at < 3:
                row = conv[at].astype(F32)
            else:
                row = sums[(at - 3) * ROWS : (at - 2) * ROWS, :INNER].astype(BF16).astype(F32)
            total = total + row * taps[k : k + 1, :]
        activ[n * ROWS : (n + 1) * ROWS, :] = silu(total).astype(BF16).astype(F32)
    act = activ[...].astype(BF16)
    low = dot(act, w_low[...]).reshape(2, BROWS // 2, RANK)
    sel = lax.dot_general(
        act, w_select[...], (((1,), (1,)), ((), ())), preferred_element_type=F32
    )
    sel = jnp.concatenate([sel, jnp.zeros((BROWS, 128 - 2 * STATE), F32)], axis=1)
    sel = sel.reshape(2, BROWS // 2, 128)
    pair_s[:, :, :RANK] = low
    pair_s[:, :, RANK:] = sel
    swap = rcopy(pair_s, pair_r, ss.at[0], rs.at[0], core)
    swap.start()
    swap.wait_recv()
    chip = pair_s[c] + pair_r[c]
    quad_s[...] = chip.astype(BF16)
    copies = [rcopy(quad_s, quad_r.at[n], ss.at[1 + n], rs.at[1 + n], others[n]) for n in range(3)]
    for copy in copies:
        copy.start()
    acc = quad_s[...].astype(F32)
    for n in range(3):
        copies[n].wait_recv()
        acc = acc + quad_r[n].astype(F32)
    full[c] = acc
    back = rcopy(full.at[c], full.at[c], ss.at[4], rs.at[4], core)
    back.start()
    rcopy(full.at[1 - c], full.at[1 - c], ss.at[4], rs.at[4], core).wait_recv()
    low_rank = full[:, :, :RANK].reshape(BROWS, RANK).astype(BF16)
    select[...] = full[:, :, RANK:].reshape(BROWS, 128)
    v = dot(low_rank, w_dt[...]) + dt_bias[...]
    step[...] = jnp.maximum(v, 0.0) + jnp.log1p(jnp.exp(-jnp.abs(v)))
    swap.wait_send()
    for copy in copies:
        copy.wait_send()
    back.wait_send()


def state_kernel(
    codes, scales, step, activ, select, sums, conv, decay_log, skip,
    gated, final, new_codes, source, last_window, output, scale_rows, rates,
):
    lane = lax.broadcasted_iota(jnp.int32, (STATE, 128), 1)
    row_of = lax.broadcasted_iota(jnp.int32, (STATE, 128), 0)
    page_lane = lax.broadcasted_iota(jnp.int32, (1, 128), 1)
    width = 4 * PAGE

    def request(i, carry):
        b_in, c_out = [], []
        for n in range(STEPS):
            row = select[pl.ds(n * ROWS + i, 1), :]
            b_in.append(jnp.sum(jnp.where(lane == row_of, row, 0.0), axis=1, keepdims=True))
            c_out.append(
                jnp.sum(jnp.where(lane == row_of + STATE, row, 0.0), axis=1, keepdims=True)
            )
        kept = [jnp.zeros((1, 128), F32) for _ in range(STEPS)]
        for part in range(INNER // width):
            cols = slice(part * width, (part + 1) * width)
            rate = rates[:, cols]
            current = codes[i, :, cols].astype(F32) * scales[pl.ds(i, 1), cols]
            for n in range(STEPS):
                at = n * ROWS + i
                dt = step[pl.ds(at, 1), cols]
                act = activ[pl.ds(at, 1), cols]
                current = jnp.exp2(dt * rate) * current + (dt * act) * b_in[n]
                output[pl.ds(at, 1), cols] = jnp.sum(current * c_out[n], axis=0, keepdims=True)
                peak = jnp.max(jnp.abs(current), axis=0, keepdims=True)
                for page in range(4):
                    here = slice(page * PAGE, (page + 1) * PAGE)
                    top = jnp.max(peak[:, here], axis=1, keepdims=True)
                    scale = (top + 1e-06).astype(BF16).astype(F32)
                    kept[n] = jnp.where(page_lane == part * 4 + page, scale, kept[n])
                    new_codes[at, :, part * width + page * PAGE : part * width + (page + 1) * PAGE] = (
                        current[:, here] * (1.0 / scale)
                    ).astype(BF16)
        for n in range(STEPS):
            scale_rows[pl.ds(n * ROWS + i, 1), :] = kept[n]
        final[i] = new_codes[(STEPS - 1) * ROWS + i]
        return carry

    rates[...] = -jnp.exp(decay_log[...]) * 1.4426950408889634
    lax.fori_loop(0, ROWS, request, 0)
    gated[...] = (
        (output[...] + skip[...] * activ[...]) * silu(sums[:, INNER:])
    ).astype(BF16)
    rows = [conv[k].astype(F32) for k in range(3)]
    rows += [sums[n * ROWS : (n + 1) * ROWS, :INNER] for n in range(STEPS)]
    for k in range(3):
        source[k * BROWS : (k + 1) * BROWS, :] = jnp.concatenate(
            rows[k + 1 : k + 1 + STEPS], axis=0
        ).astype(BF16)
        last_window[k] = rows[STEPS + k].astype(BF16)
    source[3 * BROWS :, :] = jnp.zeros((BROWS, INNER), BF16)
    source[3 * BROWS :, :128] = scale_rows[...].astype(BF16)


def middle_kernel(
    sums, conv, taps, bias, w_low, w_select, w_dt, dt_bias, codes, scales, decay_log, skip,
    gated, final, new_codes, source, last_window, step, activ, select, output, scale_rows, rates,
    *rest,
):
    rank_kernel(
        sums, conv, taps, bias, w_low, w_select, w_dt, dt_bias, step, activ, select, *rest
    )
    state_kernel(
        codes, scales, step, activ, select, sums, conv, decay_log, skip,
        gated, final, new_codes, source, last_window, output, scale_rows, rates,
    )


BACK_SCRATCH = [
    pltpu.VMEM((BLOCKS, BROWS, INNER // 2), BF16),
    pltpu.VMEM((BLOCKS, BROWS, INNER // 2), BF16),
    pltpu.VMEM((BLOCKS, BROWS, FEATS), F32),
    pltpu.SemaphoreType.DMA((2, 16)),
    pltpu.SemaphoreType.DMA((2, 16)),
]


class Gather:
    def __init__(self, axis, buf, ss, rs):
        self.axes = (axis, 1 - axis)
        self.buf, self.ss, self.rs = buf, ss, rs
        self.q, self.p = req_place(axis), req_place(1 - axis)
        self.order = [self.q, mod4(self.q - 1), mod4(self.q + 1), mod4(self.q + 2)]
        self.sent = []

    def send(self, ref, n, axis, d):
        copy = rcopy(ref, ref, self.ss.at[n], self.rs.at[n], shift_req(axis, d))
        copy.start()
        self.sent.append(copy)

    def arrived(self, ref, n):
        rcopy(ref, ref, self.ss.at[n], self.rs.at[n], shift_req(self.axes[0], 1)).wait_recv()

    def block(self, p, q):
        return self.buf.at[p * 4 + q]

    def rows(self, p, q, h):
        return self.buf.at[p * 4 + q, pl.ds(h * (BROWS // 2), BROWS // 2)]

    def start(self):
        mine = self.block(self.p, self.q)
        self.send(mine, 0, self.axes[0], 1)
        self.send(mine, 1, self.axes[0], -1)
        self.spread(0)

    def spread(self, k):
        block = self.block(self.p, self.order[k])
        self.send(block, 4 + k, self.axes[1], 1)
        self.send(block, 8 + k, self.axes[1], -1)

    def near(self):
        self.arrived(self.block(self.p, self.order[1]), 0)
        self.send(self.rows(self.p, self.order[1], 0), 2, self.axes[0], 1)
        self.spread(1)
        self.arrived(self.block(self.p, self.order[2]), 1)
        self.send(self.rows(self.p, self.order[2], 1), 3, self.axes[0], -1)
        self.spread(2)

    def last(self):
        self.arrived(self.rows(self.p, self.order[3], 0), 2)
        self.arrived(self.rows(self.p, self.order[3], 1), 3)
        self.spread(3)

    def relay(self, k):
        below, above = mod4(self.p - 1), mod4(self.p + 1)
        self.arrived(self.block(below, self.order[k]), 4 + k)
        if k < 2:
            self.send(self.block(below, self.order[k]), 12 + k, self.axes[1], 1)
        self.arrived(self.block(above, self.order[k]), 8 + k)
        if k >= 2:
            self.send(self.block(above, self.order[k]), 12 + k, self.axes[1], -1)

    def end(self, k):
        self.arrived(self.block(mod4(self.p + 2), self.order[k]), 12 + k)

    def drain(self):
        for copy in self.sent:
            copy.wait_send()


class Project:
    def __init__(self, gated, w_out, scratch):
        self.tp_bufs, rest = scratch[: len(TP_SCRATCH)], scratch[len(TP_SCRATCH) :]
        self.buf_a, self.buf_b, self.acc, gss, grs = rest
        self.gated, self.w_out = gated, w_out
        self.parts = [
            Gather(1, self.buf_a, gss.at[0], grs.at[0]),
            Gather(0, self.buf_b, gss.at[1], grs.at[1]),
        ]

    def start(self):
        r = lax.axis_index("req")
        self.acc[...] = jnp.zeros_like(self.acc)
        self.buf_a[r] = self.gated[:, :HALF]
        self.buf_b[lax.rem(r, 4) * 4 + lax.div(r, 4)] = self.gated[:, HALF:]
        for part in self.parts:
            part.start()

    def project(self, n, p, k):
        q = self.parts[n].order[k]
        if n == 0:
            self.acc[p * 4 + q] += dot(self.buf_a[p * 4 + q], self.w_out[:HALF, :])
        else:
            self.acc[q * 4 + p] += dot(self.buf_b[p * 4 + q], self.w_out[HALF:, :])

    def gather(self):
        parts = self.parts
        for part in parts:
            part.near()
        for part in parts:
            part.last()
        for k in range(4):
            for n in range(2):
                self.project(n, parts[n].p, k)
        for k in range(4):
            for part in parts:
                part.relay(k)
            for n in range(2):
                self.project(n, mod4(parts[n].p - 1), k)
                self.project(n, mod4(parts[n].p + 1), k)
        for k in range(4):
            for n in range(2):
                parts[n].end(k)
                self.project(n, mod4(parts[n].p + 2), k)

    def total(self, mixed):
        tp_sum(lambda ch: self.acc[pl.ds(2 * ch, 2)], mixed, self.tp_bufs)
        for part in self.parts:
            part.drain()


def project_kernel(gated, w_out, mixed, *scratch):
    greet(tp_partners() + req_partners())
    work = Project(gated, w_out, scratch)
    work.start()
    work.gather()
    work.total(mixed)


FAR = (2, 1, 3)


def save_scratch(room):
    return [
        pltpu.VMEM((2, 4 * room, STATE, HALF), BF16),
        pltpu.VMEM((2, 4 * room, STATE, HALF), BF16),
        pltpu.VMEM((2, 4 * room, STATE, HALF), BF16),
        pltpu.VMEM((2, 16 * room, HALF), BF16),
        pltpu.VMEM((2, 16 * room, HALF), BF16),
        pltpu.VMEM((2, 16 * room, HALF), BF16),
        pltpu.SemaphoreType.DMA((2, 2, 3, 2)),
        pltpu.SemaphoreType.DMA((2, 2, 3, 2)),
    ]


class Save:
    def __init__(self, counts, room, index, plan, codes, source, scratch):
        self.counts, self.room = counts, room
        self.index, self.plan = index, plan
        self.codes, self.source = codes, source
        self.sent, self.got1, self.got2, self.side, self.side1, self.side2, self.ss, self.rs = (
            scratch
        )

    def clear(self):
        self.side1[...] = jnp.zeros_like(self.side1)
        self.side2[...] = jnp.zeros_like(self.side2)

    def pick(self, want, rows):
        span = rows.shape[0]
        if self.room != MOST and span != self.source.shape[0]:
            row = lax.div(want, 4 * MOST) * (4 * self.room) + lax.rem(want, 4 * MOST)
            want = jnp.where(want >= 0, row, -1)
        number = lax.broadcasted_iota(jnp.int32, (span, 128), 0)
        hot = jnp.where(number == want, 1.0, 0.0).astype(BF16)
        picked = lax.dot_general(hot, rows, (((0,), (0,)), ((), ())), preferred_element_type=F32)
        return picked.astype(BF16)

    def place_of(self, at):
        at = jnp.maximum(at, 0)
        return lax.div(at, MOST) * self.room + lax.rem(at, MOST)

    def buffers(self, n):
        return ((self.got1, self.side1), (self.got2, self.side2))[n]

    def axis(self, n, h):
        return h if n == 0 else 1 - h

    def rows(self, ref, h, block, each):
        count = each * self.room
        return lambda used: ref.at[h, pl.ds(pl.multiple_of(block * count, 16 if each > 1 else 4), used)]

    def used(self, n):
        return self.counts[n], -(-4 * self.counts[n] // 16) * 16

    def copy(self, n, h, k, i):
        d = FAR[k]
        here = req_place(self.axis(n, h))
        dest, dev = mod4(here + d), shift_req(self.axis(n, h), d)
        src, dst = ((self.sent, self.side)[i], self.buffers(n)[i])
        each, used = (1, 4)[i], self.used(n)[i]
        return rcopy(
            self.rows(src, h, dest, each)(used), self.rows(dst, h, here, each)(used),
            self.ss.at[n, h, k, i], self.rs.at[n, h, k, i], dev,
        )

    def send(self, n):
        into, side_into = self.buffers(n)
        room, many = self.room, self.used(n)[1]
        order = [(k, d, h) for k, d in enumerate(FAR + (0,)) for h in range(2)]
        for k, d, h in order:
            dest = mod4(req_place(self.axis(n, h)) + d)
            keep = into if d == 0 else self.sent

            def pack(m, carry):
                at = self.index[PLAN * h + (FIRST, SECOND)[n] + dest, m]
                if n == 0:
                    row = self.codes[jnp.maximum(at, 0), :, h * HALF : (h + 1) * HALF]
                else:
                    row = self.got1[h, self.place_of(at)]
                keep[h, dest * room + m] = row
                return carry

            lax.fori_loop(0, self.counts[n], pack, 0)
            if d != 0:
                self.copy(n, h, k, 0).start()
        for k, d, h in order:
            dest = mod4(req_place(self.axis(n, h)) + d)
            keep = side_into if d == 0 else self.side
            rows = self.source[:, h * HALF : (h + 1) * HALF] if n == 0 else self.side1[h]
            want = self.plan[pl.ds(PLAN * h + (SIDE1, SIDE2)[n] + dest, 1), :]
            block = pl.ds(pl.multiple_of(dest * 4 * room, 16), many)
            keep[h, block, :] = self.pick(want, rows)[:many]
            if d != 0:
                self.copy(n, h, k, 1).start()

    def receive(self, n):
        into, side_into = self.buffers(n)
        few, many = self.used(n)
        for k, d in enumerate(FAR):
            for h in range(2):
                origin = mod4(req_place(self.axis(n, h)) - d)
                dev = shift_req(self.axis(n, h), d)
                for i, (ref, each, used) in enumerate(((into, 1, few), (side_into, 4, many))):
                    block = self.rows(ref, h, origin, each)(used)
                    rcopy(
                        block, block, self.ss.at[n, h, k, i], self.rs.at[n, h, k, i], dev
                    ).wait_recv()
        for k in range(3):
            for h in range(2):
                for i in range(2):
                    self.copy(n, h, k, i).wait_send()

    def place(self, out, windows, scale):
        def one(s, carry):
            for h in range(2):
                at = self.index[PLAN * h + LAST, s]
                row = self.got2[h, self.place_of(at)]
                out[s, :, h * HALF : (h + 1) * HALF] = jnp.where(at >= 0, row, jnp.zeros_like(row))
            return carry

        lax.fori_loop(0, SLOTS, one, 0)
        for h in range(2):
            at = self.plan[PLAN * h + LAST : PLAN * h + LAST + 1, :]
            for k in range(3):
                want = jnp.where(at >= 0, at * 4 + k, -1)
                windows[k, :, h * HALF : (h + 1) * HALF] = self.pick(want, self.side2[h])[:SLOTS]
            if h == 0:
                want = jnp.where(at >= 0, at * 4 + 3, -1)
                scale[...] = self.pick(want, self.side2[0, :, :128])[:SLOTS]


def save_partners():
    return [shift_req(axis, d) for axis in (0, 1) for d in FAR]


def save_kernel(
    counts, index, plan, codes, source, out, windows, scale, *scratch
):
    work = Save(counts, MOST, index, plan, codes, source, scratch)
    work.clear()
    greet(save_partners())
    work.send(0)
    work.receive(0)
    work.send(1)
    work.receive(1)
    work.place(out, windows, scale)


def both_kernel(
    counts, index, plan, codes, source, gated, w_out, mixed, out, windows, scale, *scratch,
):
    cut = len(TP_SCRATCH) + len(BACK_SCRATCH)
    project = Project(gated, w_out, scratch[:cut])
    save = Save(counts, ROOM, index, plan, codes, source, scratch[cut:])
    save.clear()
    greet(tp_partners() + save_partners())
    project.start()
    save.send(0)
    project.gather()
    save.receive(0)
    save.send(1)
    project.total(mixed)
    save.receive(1)
    save.place(out, windows, scale)


ROOM = 28
SAVE_COUNTS = ((20, 24), (24, 26), (MOST, MOST))


def pack_events(finish, holder, slot_index):
    packed = finish * 4096 + jnp.bitwise_and(holder, 15) * 64 + jnp.bitwise_and(slot_index, 63)
    packed = packed.reshape(STEPS, 4, 4, ROWS).transpose(2, 1, 0, 3)
    both = jnp.stack([packed, packed.transpose(1, 0, 2, 3)])
    return both.reshape(2, 4, GROUP, 1)


def per_device(
    tokens, finish, holder, slot_index, embedding, norm_gain, proj_inner, proj_gate, conv_weight,
    conv_bias, proj_low, proj_select, proj_dt, dt_bias, decay_log, skip_gain, proj_out, state_codes,
    state_scales, conv_state,
):
    ids = tokens.reshape(2, 2, BLOCKS, ROWS).transpose(0, 2, 1, 3).reshape(2, BLOCKS, PROWS, 1)
    ids = ids - lax.axis_index("tp") * embedding.shape[0]
    conv = conv_state.transpose(1, 0, 2)
    scales = jnp.repeat(state_scales.astype(F32), PAGE, axis=1)
    shape = jax.ShapeDtypeStruct
    sums, plan = vmem_call(
        front_kernel,
        [shape((BROWS, 2 * INNER), F32), shape((2 * PLAN, 128), jnp.int32)], 6, TP_PAIR * 2 + list(FRONT_SCRATCH),
        collective_id=0, has_side_effects=True,
    )(
        ids, embedding, norm_gain.reshape(1, -1), proj_inner, proj_gate,
        pack_events(finish, holder, slot_index),
    )
    half = BROWS // 2
    vmem = pl.BlockSpec(memory_space=pltpu.VMEM)
    smem = pl.BlockSpec(memory_space=pltpu.SMEM)
    gated, final, new_codes, source, last_window = vmem_call(
        middle_kernel,
        [
            shape((BROWS, INNER), BF16),
            shape((ROWS, STATE, INNER), BF16),
            shape((BROWS, STATE, INNER), BF16),
            shape((4 * BROWS, INNER), BF16),
            shape((3, ROWS, INNER), BF16),
        ],
        12,
        [
            pltpu.VMEM((BROWS, INNER), F32),
            pltpu.VMEM((BROWS, INNER), F32),
            pltpu.VMEM((BROWS, 128), F32),
            pltpu.VMEM((BROWS, INNER), F32),
            pltpu.VMEM((BROWS, 128), F32),
            pltpu.VMEM((STATE, INNER), F32),
            pltpu.VMEM((2, half, RCOLS), F32),
            pltpu.VMEM((2, half, RCOLS), F32),
            pltpu.VMEM((half, RCOLS), BF16),
            pltpu.VMEM((3, half, RCOLS), BF16),
            pltpu.VMEM((2, half, RCOLS), F32),
            pltpu.SemaphoreType.DMA((5,)),
            pltpu.SemaphoreType.DMA((5,)),
        ],
        collective_id=1, has_side_effects=True,
    )(
        sums, conv, conv_weight, conv_bias.reshape(1, -1), proj_low, proj_select, proj_dt,
        dt_bias.reshape(1, -1), state_codes, scales, decay_log, skip_gain.reshape(1, -1),
    )
    saved = [shape((SLOTS, STATE, INNER), BF16)] + [shape((3, SLOTS, INNER), BF16)] + [
        shape((SLOTS, 128), BF16)
    ]
    mixed_shape = shape((BLOCKS, BROWS, FEATS), BF16)
    back_scratch = TP_SCRATCH + BACK_SCRATCH

    def call(kernel, results, operands, scratch, number):
        return pl.pallas_call(
            kernel,
            out_shape=results,
            in_specs=[smem] + [vmem] * (len(operands) - 1),
            out_specs=[vmem] * len(results),
            scratch_shapes=scratch,
            compiler_params=pltpu.CompilerParams(
                vmem_limit_bytes=VMEM_LIMIT, collective_id=number, has_side_effects=True
            ),
        )(*operands)

    def together(n):
        def run(*operands):
            return tuple(
                call(
                    functools.partial(both_kernel, SAVE_COUNTS[n]), [mixed_shape] + saved,
                    operands, back_scratch + save_scratch(ROOM), 3 + n,
                )
            )

        return run

    def apart(*operands):
        mixed = vmem_call(
            project_kernel, mixed_shape, 2, back_scratch, collective_id=2, has_side_effects=True
        )(*operands[4:])
        rest = call(
            functools.partial(save_kernel, SAVE_COUNTS[2]), saved, operands[:4],
            save_scratch(MOST), 5,
        )
        return tuple([mixed, *rest])

    mixed, cache_codes, windows, cache_scales = lax.switch(
        plan[WHICH, 0], [together(0), together(1), apart], plan, plan, new_codes, source, gated, proj_out,
    )
    mixed = mixed.reshape(BLOCKS, STEPS, ROWS, FEATS).transpose(1, 0, 2, 3)
    mixed = mixed.reshape(STEPS, BLOCKS * ROWS, FEATS)
    last = slice((STEPS - 1) * ROWS, BROWS)
    pages = INNER // PAGE
    next_scales = source[3 * BROWS :][last, :pages]
    next_window = last_window.transpose(1, 0, 2)
    cache_window = windows.transpose(1, 0, 2)
    return (
        mixed, final, next_scales, next_window, cache_codes, cache_scales[:, :pages], cache_window,
    )


def solution(mesh):
    in_specs = (
        P(), P(), P(), P(), P("tp", "req"), P("req"), P("req", "tp"), P("req", "tp"),
        P(None, "tp"), P("tp"), P("tp", None), P(None, "tp"), P(None, "tp"), P("tp"),
        P(None, "tp"), P("tp"), P("tp", "req"), P("req", None, "tp"), P("req", "tp"),
        P("req", None, "tp"),
    )
    out_specs = (
        P(None, None, "req"), P("req", None, "tp"), P("req", "tp"), P("req", None, "tp"),
        P("req", None, "tp"), P("req", "tp"), P("req", None, "tp"),
    )
    return jax.shard_map(
        per_device, mesh=mesh, in_specs=in_specs, out_specs=out_specs, check_vma=False
    )
```

profile of v0, /device:TPU:1, one launch (start us, length us, event | category | flops | bytes accessed | tf_op | source)
XLA Modules:
  0.0 293.0 jit_solution(11096617017115966503)
XLA Ops:
  0.6 0.7 broadcast_subtract_fusion
  1.3 0.7 and_add_fusion
  2.1 0.8 copy.49
  2.8 0.1 reshape.65
  2.9 0.1 sub.14
  3.1 0.1 stack.9
  3.2 0.1 stack.10
  3.3 0.1 broadcast_in_dim.3
  3.4 0.7 copy.58
  4.2 1.2 sub.17.ids
  5.3 1.7 copy.48.events
  7.0 108.5 %shard_map.243 = (f32[96,4096]{1,0:T(8,128)}, s32[48,128]{1,0:T(8,128)S(1)}) custom-call(s32[2,16,48,1]{3,2,1,0:T(8,128)} %sub.17.ids, bf16[4096,512]{1,0:T(8,128)(2,1)} %emb.1, f32[1,512]{1,0:T(1,128)} %bitcast.40, bf16[512,2048]{1,0:T(8,128)(2,1)} %w_inner.1, bf16[512,2048]{1,0:T(8,128)(2,1)} %w_gate.1, s32[2,4,384,1]{3,2,1,0:T(8,128)} %copy.48.events), custom_call_target="tpu_custom_call" | custom-call | tf_op jit(solution)/shard_map/pallas_call | solution.py:915
  115.5 0.5 slice.19
  116.7 30.3 %shard_map.244 = (bf16[96,2048]{1,0:T(8,128)(2,1)S(1)}, bf16[24,16,2048]{2,1,0:T(8,128)(2,1)}, bf16[96,16,2048]{2,1,0:T(8,128)(2,1)}, bf16[384,2048]{1,0:T(8,128)(2,1)S(1)}, bf16[3,24,2048]{2,1,0:T(8,128)(2,1)}) custom-call(f32[96,4096]{1,0:T(8,128)} %get-tuple-element.93.sums, bf16[3,24,2048]{2,1,0:T(8,128)(2,1)} %bitcast.31, f32[4,2048]{1,0:T(4,128)} %taps.1, ...), custom_call_target="tpu_custom_call" | custom-call | tf_op jit(solution)/shard_map/pallas_call | solution.py:926
  146.9 136.9 %conditional.1 = ((bf16[16,96,512]{2,1,0:T(8,128)(2,1)}, bf16[64,16,2048]{2,1,0:T(8,128)(2,1)}, bf16[3,64,2048]{2,1,0:T(8,128)(2,1)}, bf16[64,128]{1,0:T(8,128)(2,1)S(1)})) conditional(s32[]{:T(128)} %bitcast.4, (s32[48,128]{1,0:T(8,128)S(1)}, bf16[96,16,2048]{2,1,0:T(8,128)(2,1)}, bf16[384,2048]{1,0:T(8,128)(2,1)S(1)}, ...), branch_computations={%region_0.0_spmd, %region_1.0_spmd, %region_2.0_spmd} | conditional | bytes 40 | solution.py:995
  146.9 128.2 %branch_0_fun.1 = (bf16[16,96,512]{2,1,0:T(8,128)(2,1)}, bf16[64,16,2048]{2,1,0:T(8,128)(2,1)}, bf16[3,64,2048]{2,1,0:T(8,128)(2,1)}, bf16[64,128]{1,0:T(8,128)(2,1)S(1)}) custom-call(s32[48,128]{1,0:T(8,128)S(1)} %get-tuple-element.56.index.plan, s32[48,128]{1,0:T(8,128)S(1)} %get-tuple-element.56.index.plan, ...), custom_call_target="tpu_custom_call" | custom-call | tf_op jit(solution)/shard_map/cond/branch_0_fun/pallas_call | solution.py:963
  283.8 0.7 copy.52
  284.5 0.0 copy-start.1
  284.5 0.7 copy.51
  285.2 0.0 copy-start
  285.2 2.8 copy.50
  288.0 0.0 copy-start.3
  288.0 0.0 copy-done.1
  288.0 1.1 copy.78
  289.1 0.0 copy-done.3
  289.2 0.7 copy.79
  289.9 0.0 copy-done
  289.9 0.0 copy-start.2
  289.9 2.0 copy.80
  291.9 0.0 copy-done.2
  291.9 0.9 copy.81
  (5 shorter events, 0.1 us)
Async XLA Ops:
  284.5 3.5 %copy-start.1 = (bf16[24,16,2048]{2,1,0:T(8,128)(2,1)S(1)}, bf16[24,16,2048]{2,1,0:T(8,128)(2,1)}, u32[]{:S(2)}) copy-start(bf16[24,16,2048]{2,1,0:T(8,128)(2,1)} %get-tuple-element.157) | copy-start | bytes 4718596
  285.2 4.7 %copy-start = (bf16[64,16,2048]{2,1,0:T(8,128)(2,1)S(1)}, bf16[64,16,2048]{2,1,0:T(8,128)(2,1)}, u32[]{:S(2)}) copy-start(bf16[64,16,2048]{2,1,0:T(8,128)(2,1)} %get-tuple-element.160) | copy-start | bytes 12582916
  288.0 1.1 copy-start.3
  289.9 2.0 copy-start.2
where the time goes:
time: 298 us; the launch traced here: 293 us
  Pallas kernels  267 us (90%)
  local copies, waits for them, and re-layouts  14.3 us (5%)
  loops' own time  8.65 us (3%)
    pallas_call x1, Pallas kernels, call(): pl.pallas_call(kernel, out_shape=results, in_specs=[smem] + [vmem] * (len...  128 us
    pallas_call x1, Pallas kernels, per_device(): vmem_call(front_kernel, [shape((BROWS, 2 * INNER), F32), shape((2 * PLAN,...  108 us
    pallas_call x1, Pallas kernels, per_device(): vmem_call(middle_kernel, [shape((BROWS, INNER), BF16), shape((ROWS, STATE...  30.3 us
    another operation x1, loops' own time, per_device(): lax.switch(plan[WHICH, 0], [together(0), together(1), apart], plan, plan,...  8.65 us
    unnamed x15, local copies, waits for them, and re-layouts  6.85 us

commit v1 on v0

--- a/solution.py
+++ b/solution.py
@@ -67,7 +67,7 @@
     return [(r, y * 2 + 1 - c), (r, mod4(y + 1) * 2 + c), (r, mod4(y - 1) * 2 + c)]
 
 
-def tp_steps(get, total, bufs):
+def tp_steps(get_all, total, bufs):
     half_s, half_r, part, far_s, far_r, dir_s, dir_r, com_s, com_r, ss, rs = bufs
     t = lax.axis_index("tp")
     y, c = lax.div(t, 2), lax.rem(t, 2)
@@ -86,13 +86,13 @@
     def pair(group, yy):
         return pl.ds(2 * (group * 4 + yy), 2)
 
+    get_all([(1 - c) * 4 + yy for yy in order], half_s)
     for k in range(4):
-        half_s[k] = get((1 - c) * 4 + order[k]).astype(BF16)
         send(half_s.at[k], half_r.at[k], k, core)
+    get_all([c * 4 + yy for yy in order], part)
     for k in range(4):
-        mine = get(c * 4 + order[k])
         arrived(half_r.at[k], k)
-        part[k] = mine + half_r[k].astype(F32)
+        part[k] = part[k] + half_r[k].astype(F32)
         if k == 0:
             far_s[...] = part[0].astype(BF16)
             send(far_s.at[0], far_r.at[0], 4, up)
@@ -146,7 +146,11 @@
 
 
 def tp_sum(get, total, bufs):
-    for _ in tp_steps(get, total, bufs):
+    def get_all(chunks, into):
+        for k in range(4):
+            into[k] = get(chunks[k]).astype(into.dtype)
+
+    for _ in tp_steps(get_all, total, bufs):
         pass
 
 
@@ -264,16 +268,18 @@
             lambda n: small_ss.at[g, n], lambda n: small_rs.at[g, n],
         )
 
-    def looked(self, ch):
+    def looked(self, chunks, into):
         emb = self.emb
-        want = self.ids[self.g, pl.ds(2 * ch, 2)].reshape(2 * PROWS, 1)
+        want = jnp.concatenate(
+            [self.ids[self.g, pl.ds(2 * ch, 2)].reshape(2 * PROWS, 1) for ch in chunks], axis=0
+        )
         span = 1024
-        acc = jnp.zeros((2 * PROWS, FEATS), F32)
+        acc = jnp.zeros((8 * PROWS, FEATS), F32)
         for k in range(emb.shape[0] // span):
-            lane = lax.broadcasted_iota(jnp.int32, (2 * PROWS, span), 1) + k * span
+            lane = lax.broadcasted_iota(jnp.int32, (8 * PROWS, span), 1) + k * span
             hot = jnp.where(lane == want, 1.0, 0.0).astype(BF16)
             acc = acc + dot(hot, emb[k * span : (k + 1) * span, :])
-        return acc.reshape(2, PROWS, FEATS)
+        into[...] = acc.reshape(4, 2, PROWS, FEATS).astype(into.dtype)
 
     def lookup(self):
         return tp_steps(self.looked, self.embedded, self.tp_bufs)
@@ -407,7 +413,7 @@
     need1 = jnp.max(need1, axis=1, keepdims=True)
     need2 = jnp.max(need2, axis=1, keepdims=True)
     which = jnp.full((1, 1), len(SAVE_COUNTS) - 1, jnp.int32)
-    for n in range(len(SAVE_COUNTS) - 2, -1, -1):
+    for n in range(len(SAVE_COUNTS) - 1):
         few, many = SAVE_COUNTS[n]
         which = jnp.where((need1 <= few) & (need2 <= many), n, which)
     plan[WHICH : WHICH + 1, :] = jnp.broadcast_to(which, (1, 128))
@@ -416,9 +422,16 @@
 TP_PAIR = tp_scratch(PROWS)
 
 
-def front_kernel(ids, emb, gain, w_inner, w_gate, events, out, plan, *scratch):
+def front_kernel(ids, emb, gain, inner_hbm, gate_hbm, events, out, plan, *scratch):
     cut = len(TP_PAIR)
+    w_inner, w_gate, load_sems = scratch[-3:]
     refs = (ids, emb, gain, w_inner, w_gate)
+    loads = [
+        pltpu.make_async_copy(inner_hbm, w_inner, load_sems.at[0]),
+        pltpu.make_async_copy(gate_hbm, w_gate, load_sems.at[1]),
+    ]
+    for load in loads:
+        load.start()
     one, two = (
         Front(g, refs, out, scratch[g * cut : (g + 1) * cut], scratch[2 * cut :]) for g in range(2)
     )
@@ -426,6 +439,8 @@
     for _ in one.lookup():
         pass
     one.spread()
+    for load in loads:
+        load.wait()
     one.each(lambda s: s.far())
     one.each(lambda s: s.direct())
     lookup = two.lookup()
@@ -447,12 +462,13 @@
     two.each(lambda s: s.drain())
 
 
-def vmem_call(kernel, out_shape, n_in, scratch, **params):
+def vmem_call(kernel, out_shape, n_in, scratch, in_hbm=(), **params):
     spec = pl.BlockSpec(memory_space=pltpu.VMEM)
+    hbm = pl.BlockSpec(memory_space=pl.ANY)
     return pl.pallas_call(
         kernel,
         out_shape=out_shape,
-        in_specs=[spec] * n_in,
+        in_specs=[hbm if n in in_hbm else spec for n in range(n_in)],
         out_specs=jax.tree.map(lambda _: spec, out_shape),
         scratch_shapes=scratch,
         compiler_params=pltpu.CompilerParams(vmem_limit_bytes=VMEM_LIMIT, **params),
@@ -874,14 +890,23 @@
 
 
 def both_kernel(
-    counts, index, plan, codes, source, gated, w_out, mixed, out, windows, scale, *scratch,
+    counts, index, plan, codes_hbm, source, gated, out_hbm, mixed, out, windows, scale, *scratch,
 ):
     cut = len(TP_SCRATCH) + len(BACK_SCRATCH)
+    *scratch, codes, w_out, load_sems = scratch
+    loads = [
+        pltpu.make_async_copy(codes_hbm, codes, load_sems.at[0]),
+        pltpu.make_async_copy(out_hbm, w_out, load_sems.at[1]),
+    ]
+    for load in loads:
+        load.start()
     project = Project(gated, w_out, scratch[:cut])
     save = Save(counts, ROOM, index, plan, codes, source, scratch[cut:])
     save.clear()
     greet(tp_partners() + save_partners())
     project.start()
+    for load in loads:
+        load.wait()
     save.send(0)
     project.gather()
     save.receive(0)
@@ -892,7 +917,7 @@
 
 
 ROOM = 28
-SAVE_COUNTS = ((20, 24), (24, 26), (MOST, MOST))
+SAVE_COUNTS = ((24, 26), (20, 24), (MOST, MOST))
 
 
 def pack_events(finish, holder, slot_index):
@@ -914,8 +939,12 @@
     shape = jax.ShapeDtypeStruct
     sums, plan = vmem_call(
         front_kernel,
-        [shape((BROWS, 2 * INNER), F32), shape((2 * PLAN, 128), jnp.int32)], 6, TP_PAIR * 2 + list(FRONT_SCRATCH),
-        collective_id=0, has_side_effects=True,
+        [shape((BROWS, 2 * INNER), F32), shape((2 * PLAN, 128), jnp.int32)], 6,
+        TP_PAIR * 2
+        + list(FRONT_SCRATCH)
+        + [pltpu.VMEM((FEATS, INNER), BF16)] * 2
+        + [pltpu.SemaphoreType.DMA((2,))],
+        in_hbm=(3, 4), collective_id=0, has_side_effects=True,
     )(
         ids, embedding, norm_gain.reshape(1, -1), proj_inner, proj_gate,
         pack_events(finish, holder, slot_index),
@@ -959,11 +988,15 @@
     mixed_shape = shape((BLOCKS, BROWS, FEATS), BF16)
     back_scratch = TP_SCRATCH + BACK_SCRATCH
 
-    def call(kernel, results, operands, scratch, number):
+    def call(kernel, results, operands, scratch, number, in_hbm=()):
         return pl.pallas_call(
             kernel,
             out_shape=results,
-            in_specs=[smem] + [vmem] * (len(operands) - 1),
+            in_specs=[smem]
+            + [
+                pl.BlockSpec(memory_space=pl.ANY) if n in in_hbm else vmem
+                for n in range(1, len(operands))
+            ],
             out_specs=[vmem] * len(results),
             scratch_shapes=scratch,
             compiler_params=pltpu.CompilerParams(
@@ -976,7 +1009,15 @@
             return tuple(
                 call(
                     functools.partial(both_kernel, SAVE_COUNTS[n]), [mixed_shape] + saved,
-                    operands, back_scratch + save_scratch(ROOM), 3 + n,
+                    operands,
+                    back_scratch
+                    + save_scratch(ROOM)
+                    + [
+                        pltpu.VMEM((BROWS, STATE, INNER), BF16),
+                        pltpu.VMEM((INNER, FEATS), BF16),
+                        pltpu.SemaphoreType.DMA((2,)),
+                    ],
+                    3 + n, (2, 5),
                 )
             )
 

time: 298 us -> 295 us (0.990)
  loops' own time: 8.65 us -> 1.25 us
  Pallas kernels: 267 us -> 273 us
    pallas_call x1, Pallas kernels: 128 us -> 138 us  [call(): pl.pallas_call(kernel, out_shape=results, in_specs=[smem] + [pl.BlockSpec...]
    another operation x1, loops' own time: 8.65 us -> 1.25 us  [per_device(): lax.switch(plan[WHICH, 0], [together(0), together(1), apart], plan, plan,...]
where the time goes in v1:
time: 295 us; the launch traced here: 292 us
  Pallas kernels  273 us (93%)
  local copies, waits for them, and re-layouts  14.3 us (5%)
    pallas_call x1, Pallas kernels, call(): pl.pallas_call(kernel, out_shape=results, in_specs=[smem] + [pl.BlockSpec...  138 us
    pallas_call x1, Pallas kernels, per_device(): vmem_call(front_kernel, [shape((BROWS, 2 * INNER), F32), shape((2 * PLAN,...  106 us
    pallas_call x1, Pallas kernels, per_device(): vmem_call(middle_kernel, [shape((BROWS, INNER), BF16), shape((ROWS, STATE...  29 us
    unnamed x15, local copies, waits for them, and re-layouts  6.85 us

profile of v1, /device:TPU:1, one launch (start us, length us, event | category | flops | bytes accessed | tf_op | source)
XLA Modules:
  0.0 292.1 jit_solution(9967362247855641730)
XLA Ops:
  0.6 0.7 broadcast_subtract_fusion
  1.3 0.7 and_add_fusion
  2.1 0.8 copy.49
  2.8 0.1 reshape.65
  2.9 0.1 sub.14
  3.1 0.1 stack.9
  3.2 0.1 stack.10
  3.3 0.1 broadcast_in_dim.3
  3.4 0.7 copy.58
  4.2 1.2 sub.17.ids
  5.3 1.7 copy.48.events
  7.0 105.8 %shard_map.243 = (f32[96,4096]{1,0:T(8,128)}, s32[48,128]{1,0:T(8,128)S(1)}) custom-call(s32[2,16,48,1]{3,2,1,0:T(8,128)} %sub.17.ids, bf16[4096,512]{1,0:T(8,128)(2,1)} %emb.1, f32[1,512]{1,0:T(1,128)} %bitcast.40, bf16[512,2048]{1,0:T(8,128)(2,1)} %inner_hbm.1, bf16[512,2048]{1,0:T(8,128)(2,1)} %gate_hbm.1, s32[2,4,384,1]{3,2,1,0:T(8,128)} %copy.48.events), custom_call_target="tpu_custom_call" | custom-call | tf_op jit(solution)/shard_map/pallas_call | solution.py:940
  112.8 0.5 slice.19
  114.0 29.0 %shard_map.244 = (bf16[96,2048]{1,0:T(8,128)(2,1)S(1)}, bf16[24,16,2048]{2,1,0:T(8,128)(2,1)}, bf16[96,16,2048]{2,1,0:T(8,128)(2,1)}, bf16[384,2048]{1,0:T(8,128)(2,1)S(1)}, bf16[3,24,2048]{2,1,0:T(8,128)(2,1)}) custom-call(f32[96,4096]{1,0:T(8,128)} %get-tuple-element.93.sums, bf16[3,24,2048]{2,1,0:T(8,128)(2,1)} %bitcast.31, f32[4,2048]{1,0:T(4,128)} %taps.1, ...), custom_call_target="tpu_custom_call" | custom-call | tf_op jit(solution)/shard_map/pallas_call | solution.py:955
  143.0 139.6 %conditional.1 = ((bf16[16,96,512]{2,1,0:T(8,128)(2,1)}, bf16[64,16,2048]{2,1,0:T(8,128)(2,1)}, bf16[3,64,2048]{2,1,0:T(8,128)(2,1)}, bf16[64,128]{1,0:T(8,128)(2,1)S(1)})) conditional(s32[]{:T(128)} %bitcast.4, (s32[48,128]{1,0:T(8,128)S(1)}, bf16[96,16,2048]{2,1,0:T(8,128)(2,1)}, bf16[384,2048]{1,0:T(8,128)(2,1)S(1)}, ...), branch_computations={%region_0.0_spmd, %region_1.0_spmd, %region_2.0_spmd} | conditional | bytes 40 | solution.py:1036
  143.0 138.3 %branch_0_fun.1 = (bf16[16,96,512]{2,1,0:T(8,128)(2,1)}, bf16[64,16,2048]{2,1,0:T(8,128)(2,1)}, bf16[3,64,2048]{2,1,0:T(8,128)(2,1)}, bf16[64,128]{1,0:T(8,128)(2,1)S(1)}) custom-call(s32[48,128]{1,0:T(8,128)S(1)} %get-tuple-element.56.index.plan, s32[48,128]{1,0:T(8,128)S(1)} %get-tuple-element.56.index.plan, ...), custom_call_target="tpu_custom_call" | custom-call | tf_op jit(solution)/shard_map/cond/branch_0_fun/pallas_call | solution.py:992
  282.6 0.7 copy.52
  283.3 0.0 copy-start.1
  283.3 0.7 copy.51
  284.0 0.0 copy-start
  284.0 2.8 copy.50
  286.8 0.0 copy-start.3
  286.8 0.0 copy-done.1
  286.8 1.1 copy.78
  287.9 0.0 copy-done.3
  287.9 0.7 copy.79
  288.7 0.0 copy-done
  288.7 0.0 copy-start.2
  288.7 2.0 copy.80
  290.7 0.0 copy-done.2
  290.7 0.9 copy.81
  (5 shorter events, 0.1 us)
Async XLA Ops:
  283.3 3.5 %copy-start.1 = (bf16[24,16,2048]{2,1,0:T(8,128)(2,1)S(1)}, bf16[24,16,2048]{2,1,0:T(8,128)(2,1)}, u32[]{:S(2)}) copy-start(bf16[24,16,2048]{2,1,0:T(8,128)(2,1)} %get-tuple-element.157) | copy-start | bytes 4718596
  284.0 4.7 %copy-start = (bf16[64,16,2048]{2,1,0:T(8,128)(2,1)S(1)}, bf16[64,16,2048]{2,1,0:T(8,128)(2,1)}, u32[]{:S(2)}) copy-start(bf16[64,16,2048]{2,1,0:T(8,128)(2,1)} %get-tuple-element.160) | copy-start | bytes 12582916
  286.8 1.1 copy-start.3
  288.7 2.0 copy-start.2

commit v2 on v1

--- a/solution.py
+++ b/solution.py
@@ -484,7 +484,7 @@
 
 def rank_kernel(
     sums, conv, taps, bias, w_low, w_select, w_dt, dt_bias, step, activ, select,
-    pair_s, pair_r, quad_s, quad_r, full, ss, rs,
+    pair_s, pair_r, quad_s, quad_r, full, ss, rs, loads,
 ):
     r, t = lax.axis_index("req"), lax.axis_index("tp")
     y, c = lax.div(t, 2), lax.rem(t, 2)
@@ -502,6 +502,7 @@
             total = total + row * taps[k : k + 1, :]
         activ[n * ROWS : (n + 1) * ROWS, :] = silu(total).astype(BF16).astype(F32)
     act = activ[...].astype(BF16)
+    loads[0].wait()
     low = dot(act, w_low[...]).reshape(2, BROWS // 2, RANK)
     sel = lax.dot_general(
         act, w_select[...], (((1,), (1,)), ((), ())), preferred_element_type=F32
@@ -528,6 +529,7 @@
     rcopy(full.at[1 - c], full.at[1 - c], ss.at[4], rs.at[4], core).wait_recv()
     low_rank = full[:, :, :RANK].reshape(BROWS, RANK).astype(BF16)
     select[...] = full[:, :, RANK:].reshape(BROWS, 128)
+    loads[1].wait()
     v = dot(low_rank, w_dt[...]) + dt_bias[...]
     step[...] = jnp.maximum(v, 0.0) + jnp.log1p(jnp.exp(-jnp.abs(v)))
     swap.wait_send()
@@ -595,13 +597,22 @@
 
 
 def middle_kernel(
-    sums, conv, taps, bias, w_low, w_select, w_dt, dt_bias, codes, scales, decay_log, skip,
+    sums, conv, taps, bias, low_hbm, w_select, dt_hbm, dt_bias, codes_hbm, scales, decay_log, skip,
     gated, final, new_codes, source, last_window, step, activ, select, output, scale_rows, rates,
     *rest,
 ):
+    *rest, w_low, w_dt, codes, load_sems = rest
+    loads = [
+        pltpu.make_async_copy(src, dst, load_sems.at[n])
+        for n, (src, dst) in enumerate(((low_hbm, w_low), (dt_hbm, w_dt), (codes_hbm, codes)))
+    ]
+    for load in loads:
+        load.start()
     rank_kernel(
-        sums, conv, taps, bias, w_low, w_select, w_dt, dt_bias, step, activ, select, *rest
-    )
+        sums, conv, taps, bias, w_low, w_select, w_dt, dt_bias, step, activ, select, *rest,
+        loads,
+    )
+    loads[2].wait()
     state_kernel(
         codes, scales, step, activ, select, sums, conv, decay_log, skip,
         gated, final, new_codes, source, last_window, output, scale_rows, rates,
@@ -976,7 +987,12 @@
             pltpu.VMEM((2, half, RCOLS), F32),
             pltpu.SemaphoreType.DMA((5,)),
             pltpu.SemaphoreType.DMA((5,)),
+            pltpu.VMEM((INNER, RANK), BF16),
+            pltpu.VMEM((RANK, INNER), BF16),
+            pltpu.VMEM((ROWS, STATE, INNER), BF16),
+            pltpu.SemaphoreType.DMA((3,)),
         ],
+        in_hbm=(4, 6, 8),
         collective_id=1, has_side_effects=True,
     )(
         sums, conv, conv_weight, conv_bias.reshape(1, -1), proj_low, proj_select, proj_dt,

time: 295 us -> 284 us (0.963)
  Pallas kernels: 273 us -> 261 us
    pallas_call x1, Pallas kernels: 138 us -> 127 us  [call(): pl.pallas_call(kernel, out_shape=results, in_specs=[smem] + [pl.BlockSpec...]
where the time goes in v2:
time: 284 us; the launch traced here: 280 us
  Pallas kernels  261 us (92%)
  local copies, waits for them, and re-layouts  14.3 us (5%)
    pallas_call x1, Pallas kernels, call(): pl.pallas_call(kernel, out_shape=results, in_specs=[smem] + [pl.BlockSpec...  127 us
    pallas_call x1, Pallas kernels, per_device(): vmem_call(front_kernel, [shape((BROWS, 2 * INNER), F32), shape((2 * PLAN,...  106 us
    pallas_call x1, Pallas kernels, per_device(): vmem_call(middle_kernel, [shape((BROWS, INNER), BF16), shape((ROWS, STATE...  27.6 us
    unnamed x15, local copies, waits for them, and re-layouts  6.85 us

profile of v2, /device:TPU:1, one launch (start us, length us, event | category | flops | bytes accessed | tf_op | source)
XLA Modules:
  0.0 279.9 jit_solution(14512353492659307731)
XLA Ops:
  0.6 0.7 broadcast_subtract_fusion
  1.3 0.7 and_add_fusion
  2.1 0.8 copy.49
  2.8 0.1 reshape.65
  2.9 0.1 sub.14
  3.1 0.1 stack.9
  3.2 0.1 stack.10
  3.3 0.1 broadcast_in_dim.3
  3.4 0.7 copy.58
  4.2 1.2 sub.17.ids
  5.3 1.7 copy.48.events
  7.0 106.3 %shard_map.243 = (f32[96,4096]{1,0:T(8,128)}, s32[48,128]{1,0:T(8,128)S(1)}) custom-call(s32[2,16,48,1]{3,2,1,0:T(8,128)} %sub.17.ids, bf16[4096,512]{1,0:T(8,128)(2,1)} %emb.1, f32[1,512]{1,0:T(1,128)} %bitcast.40, bf16[512,2048]{1,0:T(8,128)(2,1)} %inner_hbm.1, bf16[512,2048]{1,0:T(8,128)(2,1)} %gate_hbm.1, s32[2,4,384,1]{3,2,1,0:T(8,128)} %copy.48.events), custom_call_target="tpu_custom_call" | custom-call | tf_op jit(solution)/shard_map/pallas_call | solution.py:951
  113.3 0.5 slice.19
  114.4 27.6 %shard_map.244 = (bf16[96,2048]{1,0:T(8,128)(2,1)S(1)}, bf16[24,16,2048]{2,1,0:T(8,128)(2,1)}, bf16[96,16,2048]{2,1,0:T(8,128)(2,1)}, bf16[384,2048]{1,0:T(8,128)(2,1)S(1)}, bf16[3,24,2048]{2,1,0:T(8,128)(2,1)}) custom-call(f32[96,4096]{1,0:T(8,128)} %get-tuple-element.93.sums, bf16[3,24,2048]{2,1,0:T(8,128)(2,1)} %bitcast.31, f32[4,2048]{1,0:T(4,128)} %taps.1, ...), custom_call_target="tpu_custom_call" | custom-call | tf_op jit(solution)/shard_map/pallas_call | solution.py:966
  142.1 128.6 %conditional.1 = ((bf16[16,96,512]{2,1,0:T(8,128)(2,1)}, bf16[64,16,2048]{2,1,0:T(8,128)(2,1)}, bf16[3,64,2048]{2,1,0:T(8,128)(2,1)}, bf16[64,128]{1,0:T(8,128)(2,1)S(1)})) conditional(s32[]{:T(128)} %bitcast.4, (s32[48,128]{1,0:T(8,128)S(1)}, bf16[96,16,2048]{2,1,0:T(8,128)(2,1)}, bf16[384,2048]{1,0:T(8,128)(2,1)S(1)}, ...), branch_computations={%region_0.0_spmd, %region_1.0_spmd, %region_2.0_spmd} | conditional | bytes 40 | solution.py:1052
  142.3 127.1 %branch_1_fun.1 = (bf16[16,96,512]{2,1,0:T(8,128)(2,1)}, bf16[64,16,2048]{2,1,0:T(8,128)(2,1)}, bf16[3,64,2048]{2,1,0:T(8,128)(2,1)}, bf16[64,128]{1,0:T(8,128)(2,1)S(1)}) custom-call(s32[48,128]{1,0:T(8,128)S(1)} %get-tuple-element.61.index.plan, s32[48,128]{1,0:T(8,128)S(1)} %get-tuple-element.61.index.plan, ...), custom_call_target="tpu_custom_call" | custom-call | tf_op jit(solution)/shard_map/cond/branch_1_fun/pallas_call | solution.py:1008
  270.7 0.7 copy.52
  271.4 0.0 copy-start.1
  271.4 0.7 copy.51
  272.0 0.0 copy-start
  272.0 2.8 %copy.50 = bf16[16,4,24,512]{3,2,0,1:T(8,128)(2,1)} copy(bf16[16,4,24,512]{3,2,1,0:T(8,128)(2,1)} %bitcast.27) | data formatting | bytes 3145728 | tf_op jit(solution)/shard_map/reshape | solution.py:1055
  274.9 0.0 copy-start.3
  274.9 0.0 copy-done.1
  274.9 1.1 copy.78
  276.0 0.0 copy-done.3
  276.0 0.7 copy.79
  276.7 0.0 copy-done
  276.8 0.0 copy-start.2
  276.8 2.0 copy.80
  278.8 0.0 copy-done.2
  278.8 0.9 copy.81
  (5 shorter events, 0.1 us)
Async XLA Ops:
  271.4 3.5 %copy-start.1 = (bf16[24,16,2048]{2,1,0:T(8,128)(2,1)S(1)}, bf16[24,16,2048]{2,1,0:T(8,128)(2,1)}, u32[]{:S(2)}) copy-start(bf16[24,16,2048]{2,1,0:T(8,128)(2,1)} %get-tuple-element.157) | copy-start | bytes 4718596
  272.0 4.7 %copy-start = (bf16[64,16,2048]{2,1,0:T(8,128)(2,1)S(1)}, bf16[64,16,2048]{2,1,0:T(8,128)(2,1)}, u32[]{:S(2)}) copy-start(bf16[64,16,2048]{2,1,0:T(8,128)(2,1)} %get-tuple-element.160) | copy-start | bytes 12582916
  274.9 1.1 copy-start.3
  276.8 2.0 copy-start.2
